TPU v7x, 512 devices: a whole 4x8x8 slice. The times are simulated.
512 devices in a mesh: ctx: 16 (over z, core), head: 8 (over y_hi, x), rep: 4 (over y_lo).
Axes of the slice: x: 4, y: 8 (y_hi: 2, y_lo: 4; y = y_hi * 4 + y_lo), z: 8, core: 2. Of those that a mesh axis runs over, the one named last changes fastest.
Arguments:
- queries: bfloat16 [20480, 8192], P(('rep', 'ctx'), 'head'), parts along dimension 0, may hold values from -40 to 40
- keys: bfloat16 [20480, 1024], P(('rep', 'ctx'), 'head'), parts along dimension 0, may hold values from -25 to 25
- values: bfloat16 [20480, 1024], P(('rep', 'ctx'), 'head'), parts along dimension 0, may hold values from -6 to 6
- block_order: int32 [128], P('rep'), parts along dimension 0, may hold values from 0 to 31, each once
Outputs:
- attended: bfloat16 [20480, 8192], P(('rep', 'ctx'), 'head'), parts along dimension 0
There are 4 independent parts, one for each index of `rep`. A program takes and returns all parts, laid end to end along the dimension named above; each array names one. Nothing has to cross between parts.
Inputs may be any that keep to these rules, and one draw needn't show every extreme that they name: A permutation: stored block b, rows b * 160 to (b + 1) * 160 - 1, holds the sequence's block block_order[b].
All inputs are finite; a program needn't handle non-finite values.
Results may differ from a plain program's by a relative error of at most 0.0044.
Values may be sent and summed in bfloat16 or wider, within the bound.
No kernel may reach another device: no remote copies, remote signals or barrier semaphores. Data moves between devices by JAX's collectives and lax.ppermute only.
A program may use at most 64 MiB of HBM per device.

v0:
```python
import functools
import math

import jax
import jax.numpy as jnp
from jax import lax
from jax.experimental import pallas as pl
from jax.experimental.pallas import tpu as pltpu
from jax.sharding import PartitionSpec as P

HEAD = 128
GROUP = 8
BLOCK = 160
ROWS = 2 * BLOCK
COLS = GROUP * BLOCK
CHIPS = 8
SUMROWS = HEAD + 16
SCALE = math.log2(math.e) / math.sqrt(HEAD)
NEG = -1e30
LIMIT = 2.0**100
CHIP, NEAR_2, NEAR_1, FAR_12, NEAR_3, FAR_3_NEAR_4, FAR_4 = range(7)
WIDEST = 4 * ROWS


def dot_nt(a, b):
    return lax.dot_general(a, b, (((1,), (1,)), ((), ())), preferred_element_type=jnp.float32)


def dot_nn(a, b):
    return lax.dot_general(a, b, (((1,), (0,)), ((), ())), preferred_element_type=jnp.float32)


def sources(part, me):
    chip, core = me // 2, lax.rem(me, 2)
    up = 1 - 2 * core

    def at(steps, which):
        return lax.rem(chip + steps + CHIPS, CHIPS) * 2 + which

    def both(steps):
        return [at(steps, 0), at(steps, 1)]

    if part == CHIP:
        return both(0)
    if part == NEAR_1:
        return both(-up)
    if part == NEAR_2:
        return both(-2 * up)
    if part == FAR_12:
        return both(up) + both(2 * up)
    if part == NEAR_3:
        return both(-3 * up)
    if part == FAR_3_NEAR_4:
        return both(3 * up) + [at(4, core)]
    return [at(4, 1 - core)]


def block_positions(part, me, order_ref):
    positions = []
    for dev in sources(part, me):
        positions += [order_ref[dev * 2], order_ref[dev * 2 + 1]]
    return positions


def stage(part, *refs):
    first, last = part == CHIP, part == FAR_4
    if first:
        me_ref, order_in, q_ref, kv_ref, qs_ref, seen_ref, m_out, acc_out, vt, order_ref, product, sems = refs
        stab = m_out
    elif last:
        qs_ref, seen_ref, stab, acc_in, kv_ref, o_ref, vt, seen_t, acc_out, m_out = refs
    else:
        qs_ref, seen_ref, stab, acc_in, kv_ref, m_out, acc_out, vt, seen_t = refs
    span = kv_ref.shape[0]

    if first:
        copies = [(order_in, order_ref)]
        for a in range(2):
            for h in range(GROUP):
                copies.append(
                    (
                        q_ref.at[pl.ds(a * BLOCK, BLOCK), pl.ds(h * HEAD, HEAD)],
                        qs_ref.at[pl.ds(a * COLS + h * BLOCK, BLOCK), :],
                    )
                )
        copies = [pltpu.make_async_copy(src, dst, sems.at[i]) for i, (src, dst) in enumerate(copies)]
        for copy in copies:
            copy.start()

    values_t = kv_ref[:, HEAD:].astype(jnp.float32).T

    if first:
        vt[:HEAD, :] = values_t.astype(jnp.bfloat16)
        vt[HEAD:, :] = jnp.ones((SUMROWS - HEAD, span), jnp.bfloat16)
        copies[0].wait()
        me = me_ref[0]
        lane = lax.broadcasted_iota(jnp.int32, (1, WIDEST), 1)
        seen_ref[...] = jnp.zeros(seen_ref.shape, jnp.float32)
        for other in range(NEAR_2, FAR_4 + 1):
            lane_pos = jnp.zeros((1, WIDEST), jnp.int32)
            for j, pos in enumerate(block_positions(other, me, order_ref)):
                lane_pos = jnp.where(lane >= j * BLOCK, pos, lane_pos)
            for a in range(2):
                seen = jnp.where(lane_pos < order_ref[me * 2 + a], 1.0, 0.0)
                seen_ref[2 * other + a : 2 * other + a + 1, :] = seen
        row = lax.broadcasted_iota(jnp.int32, (span, 1), 0)
        key_pos = jnp.zeros((span, 1), jnp.int32)
        for j, pos in enumerate(block_positions(part, me, order_ref)):
            key_pos = jnp.where(row >= j * BLOCK, (pos - j) * BLOCK, key_pos)
        key_pos = key_pos + row
        for copy in copies[1:]:
            copy.wait()
        mine = lax.rem(me, 2) * ROWS
        for a in range(2):
            key_rows = kv_ref[pl.ds(pl.multiple_of(mine + a * BLOCK, BLOCK), BLOCK), :HEAD]
            for h in range(GROUP):
                rows = slice(a * COLS + h * BLOCK, a * COLS + (h + 1) * BLOCK)
                product[rows, :] = qs_ref[rows, :] * key_rows
        for c in range(0, 2 * COLS, 256):
            diag = dot_nt(jnp.ones((8, HEAD), jnp.bfloat16), product[c : c + 256, :])
            m_out[:, c : c + 256] = diag[:1] * SCALE

    def scores(a):
        return dot_nt(kv_ref[:, :HEAD], qs_ref[a * COLS : (a + 1) * COLS, :])

    over = jnp.zeros((1, 256), jnp.float32)
    ahead = scores(0)
    for a in range(2):
        cols = slice(a * COLS, (a + 1) * COLS)
        s, ahead = ahead, scores(1) if a == 0 else None
        p = jnp.exp2(s * SCALE - stab[:, cols])
        if first:
            token = lax.rem(lax.broadcasted_iota(jnp.int32, (1, COLS), 1), BLOCK) + order_ref[me * 2 + a] * BLOCK
            p = jnp.where(key_pos <= token, p, 0.0)
        else:
            seen = seen_ref[2 * part + a : 2 * part + a + 1, :span]
            vt[:HEAD, :] = (values_t * seen).astype(jnp.bfloat16)
            vt[HEAD:, :] = jnp.broadcast_to(seen, (SUMROWS - HEAD, span)).astype(jnp.bfloat16)
        new = dot_nn(vt[...], p.astype(jnp.bfloat16))
        if not first:
            new = new + acc_in[:, cols]
            m_out[:, cols] = stab[:, cols]
        acc_out[:, cols] = new
        mass = jnp.where(new[HEAD : HEAD + 1] <= LIMIT, 0.0, 1.0)
        for i in range(0, COLS, 256):
            over = over + mass[:, i : i + 256]

    @pl.when(jnp.sum(over) > 0.0)
    def _():
        if not first:
            seen_t[...] = seen_ref[...].T

        def tile(t, carry):
            a = t // (COLS // 256)
            cols = pl.ds(pl.multiple_of(t * 256, 256), 256)
            acc_out[:, cols] = jnp.zeros((SUMROWS, 256), jnp.float32) if first else acc_in[:, cols]
            m_out[:, cols] = stab[:, cols]

            def block(j, carry):
                rows = pl.ds(pl.multiple_of(j * BLOCK, BLOCK), BLOCK)
                s = dot_nt(kv_ref[rows, :HEAD], qs_ref[cols, :]) * SCALE
                if first:
                    col = (t - a * (COLS // 256)) * 256
                    token = lax.rem(lax.broadcasted_iota(jnp.int32, (1, 256), 1) + col, BLOCK)
                    key = lax.broadcasted_iota(jnp.int32, (BLOCK, 1), 0)
                    ahead = order_ref[me * 2 + a] - order_ref[me // 2 * 4 + j]
                    visible = key <= token + ahead * BLOCK
                else:
                    visible = jnp.where(a == 0, seen_t[rows, 2 * part : 2 * part + 1], seen_t[rows, 2 * part + 1 : 2 * part + 2])
                    visible = jnp.broadcast_to(visible, s.shape) > 0.5
                s = jnp.where(visible, s, NEG)
                m = m_out[:, cols]
                peak = jnp.maximum(m, jnp.max(s, axis=0, keepdims=True))
                p = jnp.exp2(s - peak).astype(jnp.bfloat16)
                value = jnp.concatenate(
                    [kv_ref[rows, HEAD:].astype(jnp.float32).T, jnp.ones((SUMROWS - HEAD, BLOCK), jnp.float32)], 0
                )
                acc_out[:, cols] = acc_out[:, cols] * jnp.exp2(m - peak) + dot_nn(value.astype(jnp.bfloat16), p)
                m_out[:, cols] = peak
                return carry

            return lax.fori_loop(0, span // BLOCK, block, carry)

        lax.fori_loop(0, 2 * COLS // 256, tile, 0)

    if last:
        for a in range(2):
            sums = acc_out[:, a * COLS : (a + 1) * COLS]
            full = (sums[:HEAD] * (1.0 / sums[HEAD : HEAD + 1])).T.astype(jnp.bfloat16)
            for h in range(GROUP):
                o_ref[a * BLOCK : (a + 1) * BLOCK, h * HEAD : (h + 1) * HEAD] = full[h * BLOCK : (h + 1) * BLOCK, :]


SUMS = jax.ShapeDtypeStruct((SUMROWS, 2 * COLS), jnp.float32)
TOPS = jax.ShapeDtypeStruct((1, 2 * COLS), jnp.float32)
LAID = jax.ShapeDtypeStruct((2 * COLS, HEAD), jnp.bfloat16)
SEEN = jax.ShapeDtypeStruct((16, WIDEST), jnp.float32)
VMEM = pl.BlockSpec(memory_space=pltpu.VMEM)
SMEM = pl.BlockSpec(memory_space=pltpu.SMEM)
ANY = pl.BlockSpec(memory_space=pl.ANY)


def run_stage(part, given, kv):
    span = kv.shape[0]
    scratch = [pltpu.VMEM((SUMROWS, span), jnp.bfloat16)]
    out, specs = (TOPS, SUMS), [VMEM] * 4
    if part == CHIP:
        out, specs = (LAID, SEEN, TOPS, SUMS), [SMEM, ANY, ANY]
        scratch += [pltpu.SMEM(given[1].shape, jnp.int32), pltpu.VMEM(LAID.shape, jnp.bfloat16)]
        scratch += [pltpu.SemaphoreType.DMA((1 + 2 * GROUP,))]
    else:
        scratch += [pltpu.VMEM(SEEN.shape[::-1], jnp.float32)]
    if part == FAR_4:
        out = jax.ShapeDtypeStruct((ROWS, GROUP * HEAD), jnp.bfloat16)
        scratch += [pltpu.VMEM(SUMS.shape, jnp.float32), pltpu.VMEM(TOPS.shape, jnp.float32)]
    pairs = 1 if part == NEAR_3 else span * 2 * COLS
    result = pl.pallas_call(
        functools.partial(stage, part),
        out_shape=out,
        in_specs=specs + [VMEM],
        out_specs=jax.tree.map(lambda _: VMEM, out),
        scratch_shapes=scratch,
        compiler_params=pltpu.CompilerParams(vmem_limit_bytes=40 * 2**20),
        cost_estimate=pl.CostEstimate(flops=pairs * HEAD * 4, bytes_accessed=pairs, transcendentals=pairs),
    )(*given, kv)
    if part in (CHIP, FAR_4):
        return result
    return (*given[:2], *result)


def both_cores(block):
    pairs = [[2 * i, 2 * i + 1] for i in range(CHIPS)]
    return lax.all_gather(block, "ctx", tiled=True, axis_index_groups=pairs)


def other_core(block):
    return lax.ppermute(block, "ctx", [(i, i ^ 1) for i in range(2 * CHIPS)])


def away(block, hops):
    route = []
    for chip in range(CHIPS):
        route.append((chip * 2, (chip + hops) % CHIPS * 2))
        route.append((chip * 2 + 1, (chip - hops) % CHIPS * 2 + 1))
    return lax.ppermute(block, "ctx", route)


def after(block, state):
    block, _ = lax.optimization_barrier((block, state[-1]))
    return block


def per_device(queries, keys, values, block_order):
    me = lax.axis_index("ctx")
    chip = both_cores(jnp.concatenate([keys, values], axis=1))
    near_2 = away(chip, 2)
    near_1 = away(chip, 1)
    state = run_stage(CHIP, (me.astype(jnp.int32).reshape(1), block_order, queries), chip)
    near_2 = after(near_2, state)
    near_3 = away(near_2, 1)
    state = run_stage(NEAR_2, state, near_2)
    near_2 = after(near_2, state)
    near_1 = after(near_1, state)
    far_12 = other_core(jnp.concatenate([near_1, near_2], axis=0))
    state = run_stage(NEAR_1, state, near_1)
    half = lax.dynamic_slice_in_dim(after(near_2, state), me % 2 * ROWS, ROWS, 0)
    near_4 = away(half, 2)
    state = run_stage(FAR_12, state, far_12)
    near_3 = after(near_3, state)
    far_3 = other_core(near_3)
    state = run_stage(NEAR_3, state, near_3)
    near_4 = after(near_4, state)
    far_4 = other_core(near_4)
    state = run_stage(FAR_3_NEAR_4, state, jnp.concatenate([far_3, near_4], axis=0))
    return run_stage(FAR_4, state, far_4)


def solution(mesh):
    placed = P(("rep", "ctx"), "head")
    return jax.shard_map(
        per_device,
        mesh=mesh,
        in_specs=(placed, placed, placed, P("rep")),
        out_specs=placed,
        check_vma=False,
    )
```

profile of v0, /device:TPU:49, one launch (start us, length us, event | category | flops | bytes accessed | tf_op | source)
XLA Modules:
  0.0 82.5 jit_solution(5974838134647683974)
XLA Ops:
  0.0 0.9 %pad_maximum_fusion.2 = bf16[320,256]{1,0:T(8,128)(2,1)S(1)} fusion(bf16[320,128]{1,0:T(8,128)(2,1)} %param.6, bf16[320,128]{1,0:T(8,128)(2,1)} %param.5), kind=kLoop, calls=%fused_computation.2 | loop fusion | flops 327680 | bytes 327680 | tf_op jit(solution)/shard_map/concatenate | solution.py:255
  0.9 2.4 %all_gather.3.refs_3_ = bf16[640,256]{1,0:T(8,128)(2,1)S(1)} all-gather(bf16[320,256]{1,0:T(8,128)(2,1)S(1)} %pad_maximum_fusion.2), channel_id=1, replica_groups={{0,32},{64,96},{128,160},{192,224},{256,288},{320,352},{384,416},{448,4..., dimensions={0}, use_global_device_ids=true | all-gather | bytes 491520 | tf_op jit(solution)/shard_map/all_gather | solution.py:233
  3.3 10.6 %collective-permute-start = (bf16[640,256]{1,0:T(8,128)(2,1)S(1)}, bf16[640,256]{1,0:T(8,128)(2,1)S(1)}, u32[]{:S(2)}, u32[]{:S(2)}) collective-permute-start(bf16[640,256]{1,0:T(8,128)(2,1)S(1)} %all_gather.3.refs_3_), channel_id=1, source_target_pairs={{0,128},{32,416},{64,192},{96,480},{128,256},{160,32},{192,320},{2... | collective-permute-start | bytes 983048 | tf_op jit(solution)/shard_map/ppermute | solution.py:245
  14.0 2.2 %collective-permute-start.1 = (bf16[640,256]{1,0:T(8,128)(2,1)S(1)}, bf16[640,256]{1,0:T(8,128)(2,1)S(1)}, u32[]{:S(2)}, u32[]{:S(2)}) collective-permute-start(bf16[640,256]{1,0:T(8,128)(2,1)S(1)} %all_gather.3.refs_3_), channel_id=1, source_target_pairs={{0,64},{32,480},{64,128},{96,32},{128,192},{160,96},{192,256},{224... | collective-permute-start | bytes 983048 | tf_op jit(solution)/shard_map/ppermute | solution.py:245
  16.1 0.0 copy-start
  16.2 1.1 %copy-done = bf16[320,1024]{1,0:T(8,128)(2,1)S(1)} copy-done((bf16[320,1024]{1,0:T(8,128)(2,1)S(1)}, bf16[320,1024]{1,0:T(8,128)(2,1)}, u32[]{:S(2)}) %copy-start) | copy-done | bytes 655384
  17.2 0.0 copy-start.1
  17.2 0.7 copy-done.1
  17.9 18.5 %shard_map.46 = (bf16[2560,128]{1,0:T(8,128)(2,1)S(1)}, f32[16,1280]{1,0:T(8,128)S(1)}, f32[1,2560]{1,0:T(1,128)S(1)}, f32[144,2560]{1,0:T(8,128)S(1)}) custom-call(s32[1]{0:T(128)} %bitcast.refs_0_, s32[32]{0:T(128)S(1)} %copy-done.1, bf16[320,1024]{1,0:T(8,128)(2,1)S(1)} %copy-done, bf16[640,256]{1,0:T(8,128)(2,1)S(1)} %all_gather.3.refs_3_), custom_call_target="tpu_custom_call" | custom-call | flops 838860800 | bytes 1638400 | tf_op jit(solution)/shard_map/pallas_call | solution.py:217
  36.4 0.0 collective-permute-done.refs_4_
  36.5 1.9 %shard_map.47 = (f32[1,2560]{1,0:T(1,128)S(1)}, f32[144,2560]{1,0:T(8,128)S(1)}) custom-call(bf16[2560,128]{1,0:T(8,128)(2,1)S(1)} %get-tuple-element.25.refs_0_, f32[16,1280]{1,0:T(8,128)S(1)} %get-tuple-element.26.refs_1_, f32[1,2560]{1,0:T(1,128)S(1)} %get-tuple-element.27.refs_2_, f32[144,2560]{1,0:T(8,128)S(1)} %get-tuple-element.28.refs_3_, ...), custom_call_target="tpu_custom_call" | custom-call | flops 838860800 | bytes 1638400 | tf_op jit(solution)/shard_map/pallas_call | solution.py:217
  38.3 0.0 collective-permute-done.1.refs_4_
  38.4 15.9 %collective-permute-start.2 = (bf16[1280,256]{1,0:T(8,128)(2,1)S(1)}, bf16[1280,256]{1,0:T(8,128)(2,1)S(1)}, u32[]{:S(2)}, u32[]{:S(2)}) collective-permute-start(bf16[1280,256]{1,0:T(8,128)(2,1)S(1)} %pad_maximum_fusion), channel_id=1, source_target_pairs={{0,32},{32,0},{64,96},{96,64},{128,160},{160,128},{192,224},{224,1... | collective-permute-start | bytes 1966088 | tf_op jit(solution)/shard_map/ppermute | solution.py:237
  54.3 1.9 %collective-permute-start.3 = (bf16[640,256]{1,0:T(8,128)(2,1)S(1)}, bf16[640,256]{1,0:T(8,128)(2,1)S(1)}, u32[]{:S(2)}, u32[]{:S(2)}) collective-permute-start(bf16[640,256]{1,0:T(8,128)(2,1)S(1)} %collective-permute-done.refs_4_), channel_id=1, source_target_pairs={{0,64},{32,480},{64,128},{96,32},{128,192},{160,96},{192,256},{224... | collective-permute-start | bytes 983048 | tf_op jit(solution)/shard_map/ppermute | solution.py:245
  56.2 1.8 %shard_map.48 = (f32[1,2560]{1,0:T(1,128)S(1)}, f32[144,2560]{1,0:T(8,128)S(1)}) custom-call(bf16[2560,128]{1,0:T(8,128)(2,1)S(1)} %get-tuple-element.25.refs_0_, f32[16,1280]{1,0:T(8,128)S(1)} %get-tuple-element.26.refs_1_, f32[1,2560]{1,0:T(1,128)S(1)} %get-tuple-element.30.refs_2_, f32[144,2560]{1,0:T(8,128)S(1)} %get-tuple-element.31.refs_3_, ...), custom_call_target="tpu_custom_call" | custom-call | flops 838860800 | bytes 1638400 | tf_op jit(solution)/shard_map/pallas_call | solution.py:217
  58.0 0.0 collective-permute-done.2.refs_4_
  58.0 3.1 %shard_map.49 = (f32[1,2560]{1,0:T(1,128)S(1)}, f32[144,2560]{1,0:T(8,128)S(1)}) custom-call(bf16[2560,128]{1,0:T(8,128)(2,1)S(1)} %get-tuple-element.25.refs_0_, f32[16,1280]{1,0:T(8,128)S(1)} %get-tuple-element.26.refs_1_, f32[1,2560]{1,0:T(1,128)S(1)} %get-tuple-element.33.refs_2_, f32[144,2560]{1,0:T(8,128)S(1)} %get-tuple-element.34.refs_3_, ...), custom_call_target="tpu_custom_call" | custom-call | flops 1677721600 | bytes 3276800 | tf_op jit(solution)/shard_map/pallas_call | solution.py:217
  61.2 1.2 %collective-permute-done.3.refs_4_ = bf16[640,256]{1,0:T(8,128)(2,1)S(1)} collective-permute-done((bf16[640,256]{1,0:T(8,128)(2,1)S(1)}, bf16[640,256]{1,0:T(8,128)(2,1)S(1)}, u32[]{:S(2)}, u32[]{:S(2)}) %collective-permute-start.3) | collective-permute-done | bytes 327712 | tf_op jit(solution)/shard_map/ppermute | solution.py:245
  62.4 4.0 %collective-permute-start.4 = (bf16[640,256]{1,0:T(8,128)(2,1)S(1)}, bf16[640,256]{1,0:T(8,128)(2,1)S(1)}, u32[]{:S(2)}, u32[]{:S(2)}) collective-permute-start(bf16[640,256]{1,0:T(8,128)(2,1)S(1)} %collective-permute-done.3.refs_4_), channel_id=1, source_target_pairs={{0,32},{32,0},{64,96},{96,64},{128,160},{160,128},{192,224},{224,1... | collective-permute-start | bytes 983048 | tf_op jit(solution)/shard_map/ppermute | solution.py:237
  66.4 1.9 %collective-permute-start.5 = (bf16[320,256]{1,0:T(8,128)(2,1)S(1)}, bf16[320,256]{1,0:T(8,128)(2,1)S(1)}, u32[]{:S(2)}, u32[]{:S(2)}) collective-permute-start(bf16[320,256]{1,0:T(8,128)(2,1)S(1)} %constant_dynamic-slice_fusion), channel_id=1, source_target_pairs={{0,128},{32,416},{64,192},{96,480},{128,256},{160,32},{192,320},{2... | collective-permute-start | bytes 491528 | tf_op jit(solution)/shard_map/ppermute | solution.py:245
  68.3 2.0 %shard_map.50 = (f32[1,2560]{1,0:T(1,128)S(1)}, f32[144,2560]{1,0:T(8,128)S(1)}) custom-call(bf16[2560,128]{1,0:T(8,128)(2,1)S(1)} %get-tuple-element.25.refs_0_, f32[16,1280]{1,0:T(8,128)S(1)} %get-tuple-element.26.refs_1_, f32[1,2560]{1,0:T(1,128)S(1)} %get-tuple-element.36.refs_2_, f32[144,2560]{1,0:T(8,128)S(1)} %get-tuple-element.37.refs_3_, ...), custom_call_target="tpu_custom_call" | custom-call | flops 512 | bytes 1 | tf_op jit(solution)/shard_map/pallas_call | solution.py:217
  70.3 3.4 %collective-permute-done.5 = bf16[320,256]{1,0:T(8,128)(2,1)S(1)} collective-permute-done((bf16[320,256]{1,0:T(8,128)(2,1)S(1)}, bf16[320,256]{1,0:T(8,128)(2,1)S(1)}, u32[]{:S(2)}, u32[]{:S(2)}) %collective-permute-start.5) | collective-permute-done | bytes 163872 | tf_op jit(solution)/shard_map/ppermute | solution.py:245
  73.7 3.9 %collective-permute-start.6 = (bf16[320,256]{1,0:T(8,128)(2,1)S(1)}, bf16[320,256]{1,0:T(8,128)(2,1)S(1)}, u32[]{:S(2)}, u32[]{:S(2)}) collective-permute-start(bf16[320,256]{1,0:T(8,128)(2,1)S(1)} %collective-permute-done.5), channel_id=1, source_target_pairs={{0,32},{32,0},{64,96},{96,64},{128,160},{160,128},{192,224},{224,1... | collective-permute-start | bytes 491528 | tf_op jit(solution)/shard_map/ppermute | solution.py:237
  77.6 0.0 collective-permute-done.4
  77.7 2.6 %shard_map.51 = (f32[1,2560]{1,0:T(1,128)S(1)}, f32[144,2560]{1,0:T(8,128)S(1)}) custom-call(bf16[2560,128]{1,0:T(8,128)(2,1)S(1)} %get-tuple-element.25.refs_0_, f32[16,1280]{1,0:T(8,128)S(1)} %get-tuple-element.26.refs_1_, f32[1,2560]{1,0:T(1,128)S(1)} %get-tuple-element.39.refs_2_, f32[144,2560]{1,0:T(8,128)S(1)} %get-tuple-element.40.refs_3_, ...), custom_call_target="tpu_custom_call" | custom-call | flops 1258291200 | bytes 2457600 | tf_op jit(solution)/shard_map/pallas_call | solution.py:217
  80.3 0.0 collective-permute-done.6.refs_4_
  80.3 2.3 %shard_map.52 = bf16[320,1024]{1,0:T(8,128)(2,1)} custom-call(bf16[2560,128]{1,0:T(8,128)(2,1)S(1)} %get-tuple-element.25.refs_0_, f32[16,1280]{1,0:T(8,128)S(1)} %get-tuple-element.26.refs_1_, f32[1,2560]{1,0:T(1,128)S(1)} %get-tuple-element.43.refs_2_, f32[144,2560]{1,0:T(8,128)S(1)} %get-tuple-element.44.refs_3_, ...), custom_call_target="tpu_custom_call" | custom-call | flops 419430400 | bytes 819200 | tf_op jit(solution)/shard_map/pallas_call | solution.py:217
  (3 shorter events, 0.1 us)
Async XLA Ops:
  3.3 33.1 %collective-permute-start = (bf16[640,256]{1,0:T(8,128)(2,1)S(1)}, bf16[640,256]{1,0:T(8,128)(2,1)S(1)}, u32[]{:S(2)}, u32[]{:S(2)}) collective-permute-start(bf16[640,256]{1,0:T(8,128)(2,1)S(1)} %all_gather.3.refs_3_), channel_id=1, source_target_pairs={{0,128},{32,416},{64,192},{96,480},{128,256},{160,32},{192,320},{2... | collective-permute-start | bytes 983048 | tf_op jit(solution)/shard_map/ppermute | solution.py:245
  14.0 24.4 %collective-permute-start.1 = (bf16[640,256]{1,0:T(8,128)(2,1)S(1)}, bf16[640,256]{1,0:T(8,128)(2,1)S(1)}, u32[]{:S(2)}, u32[]{:S(2)}) collective-permute-start(bf16[640,256]{1,0:T(8,128)(2,1)S(1)} %all_gather.3.refs_3_), channel_id=1, source_target_pairs={{0,64},{32,480},{64,128},{96,32},{128,192},{160,96},{192,256},{224... | collective-permute-start | bytes 983048 | tf_op jit(solution)/shard_map/ppermute | solution.py:245
  16.1 1.1 %copy-start = (bf16[320,1024]{1,0:T(8,128)(2,1)S(1)}, bf16[320,1024]{1,0:T(8,128)(2,1)}, u32[]{:S(2)}) copy-start(bf16[320,1024]{1,0:T(8,128)(2,1)} %refs_2_.1) | copy-start | bytes 1966084
  17.2 0.7 copy-start.1
  38.4 19.7 %collective-permute-start.2 = (bf16[1280,256]{1,0:T(8,128)(2,1)S(1)}, bf16[1280,256]{1,0:T(8,128)(2,1)S(1)}, u32[]{:S(2)}, u32[]{:S(2)}) collective-permute-start(bf16[1280,256]{1,0:T(8,128)(2,1)S(1)} %pad_maximum_fusion), channel_id=1, source_target_pairs={{0,32},{32,0},{64,96},{96,64},{128,160},{160,128},{192,224},{224,1... | collective-permute-start | bytes 1966088 | tf_op jit(solution)/shard_map/ppermute | solution.py:237
  54.3 8.1 %collective-permute-start.3 = (bf16[640,256]{1,0:T(8,128)(2,1)S(1)}, bf16[640,256]{1,0:T(8,128)(2,1)S(1)}, u32[]{:S(2)}, u32[]{:S(2)}) collective-permute-start(bf16[640,256]{1,0:T(8,128)(2,1)S(1)} %collective-permute-done.refs_4_), channel_id=1, source_target_pairs={{0,64},{32,480},{64,128},{96,32},{128,192},{160,96},{192,256},{224... | collective-permute-start | bytes 983048 | tf_op jit(solution)/shard_map/ppermute | solution.py:245
  62.4 15.3 %collective-permute-start.4 = (bf16[640,256]{1,0:T(8,128)(2,1)S(1)}, bf16[640,256]{1,0:T(8,128)(2,1)S(1)}, u32[]{:S(2)}, u32[]{:S(2)}) collective-permute-start(bf16[640,256]{1,0:T(8,128)(2,1)S(1)} %collective-permute-done.3.refs_4_), channel_id=1, source_target_pairs={{0,32},{32,0},{64,96},{96,64},{128,160},{160,128},{192,224},{224,1... | collective-permute-start | bytes 983048 | tf_op jit(solution)/shard_map/ppermute | solution.py:237
  66.4 7.3 %collective-permute-start.5 = (bf16[320,256]{1,0:T(8,128)(2,1)S(1)}, bf16[320,256]{1,0:T(8,128)(2,1)S(1)}, u32[]{:S(2)}, u32[]{:S(2)}) collective-permute-start(bf16[320,256]{1,0:T(8,128)(2,1)S(1)} %constant_dynamic-slice_fusion), channel_id=1, source_target_pairs={{0,128},{32,416},{64,192},{96,480},{128,256},{160,32},{192,320},{2... | collective-permute-start | bytes 491528 | tf_op jit(solution)/shard_map/ppermute | solution.py:245
  73.7 6.6 %collective-permute-start.6 = (bf16[320,256]{1,0:T(8,128)(2,1)S(1)}, bf16[320,256]{1,0:T(8,128)(2,1)S(1)}, u32[]{:S(2)}, u32[]{:S(2)}) collective-permute-start(bf16[320,256]{1,0:T(8,128)(2,1)S(1)} %collective-permute-done.5), channel_id=1, source_target_pairs={{0,32},{32,0},{64,96},{96,64},{128,160},{160,128},{192,224},{224,1... | collective-permute-start | bytes 491528 | tf_op jit(solution)/shard_map/ppermute | solution.py:237
where the time goes:
time: 82.9 us; the launch traced here: 82.5 us
  starting transfers between devices  40.4 us (49%)
  Pallas kernels  32.2 us (39%)
  waiting for transfers between devices  4.61 us (6%)
  blocking collectives  2.35 us (3%)
  local copies, waits for them, and re-layouts  1.76 us (2%)
  other arithmetic  1.02 us (1%)
    pallas_call x7, Pallas kernels, run_stage(): pl.pallas_call(functools.partial(stage, part), out_shape=out, in_specs=sp...  32.2 us
    ppermute x3, starting transfers between devices, other_core(): return lax.ppermute(block, 'ctx', [(i, i ^ 1) for i in range(2 * CHIPS)])  23.8 us
    ppermute x4, starting transfers between devices, away(): return lax.ppermute(block, 'ctx', route)  16.7 us
    ppermute x4, waiting for transfers between devices, away(): return lax.ppermute(block, 'ctx', route)  4.6 us
    all_gather x1, blocking collectives, both_cores(): return lax.all_gather(block, 'ctx', tiled=True, axis_index_groups=pairs)  2.35 us
    unnamed x4, local copies, waits for them, and re-layouts  1.74 us
  transfers between devices with their start and end apart: 7, of which 2 were waited for; matrix products, arithmetic and copies ran while one was open for 0% of the time, Pallas kernels for 36%

commit v1 on v0

--- a/solution.py
+++ b/solution.py
@@ -213,7 +213,6 @@
     if part == FAR_4:
         out = jax.ShapeDtypeStruct((ROWS, GROUP * HEAD), jnp.bfloat16)
         scratch += [pltpu.VMEM(SUMS.shape, jnp.float32), pltpu.VMEM(TOPS.shape, jnp.float32)]
-    pairs = 1 if part == NEAR_3 else span * 2 * COLS
     result = pl.pallas_call(
         functools.partial(stage, part),
         out_shape=out,
@@ -221,7 +220,7 @@
         out_specs=jax.tree.map(lambda _: VMEM, out),
         scratch_shapes=scratch,
         compiler_params=pltpu.CompilerParams(vmem_limit_bytes=40 * 2**20),
-        cost_estimate=pl.CostEstimate(flops=pairs * HEAD * 4, bytes_accessed=pairs, transcendentals=pairs),
+        cost_estimate=pl.CostEstimate(flops=1, bytes_accessed=1, transcendentals=0),
     )(*given, kv)
     if part in (CHIP, FAR_4):
         return result

time: 82.9 us -> 96.4 us (1.16)
  the two profiles are of different devices: /device:TPU:49 before, /device:TPU:39 now
where the time goes in v1:
time: 96.4 us; the launch traced here: 96 us
  waiting for transfers between devices  32.9 us (34%)
  Pallas kernels  32.2 us (33%)
  starting transfers between devices  25.6 us (27%)
  blocking collectives  2.35 us (2%)
  local copies, waits for them, and re-layouts  1.76 us (2%)
  other arithmetic  1.02 us (1%)
    ppermute x4, waiting for transfers between devices, away(): return lax.ppermute(block, 'ctx', route)  32.9 us
    pallas_call x7, Pallas kernels, run_stage(): pl.pallas_call(functools.partial(stage, part), out_shape=out, in_specs=sp...  32.2 us
    ppermute x4, starting transfers between devices, away(): return lax.ppermute(block, 'ctx', route)  16.9 us
    ppermute x3, starting transfers between devices, other_core(): return lax.ppermute(block, 'ctx', [(i, i ^ 1) for i in range(2 * CHIPS)])  8.69 us
    all_gather x1, blocking collectives, both_cores(): return lax.all_gather(block, 'ctx', tiled=True, axis_index_groups=pairs)  2.35 us
  transfers between devices with their start and end apart: 7, of which 2 were waited for; matrix products, arithmetic and copies ran while one was open for 0% of the time, Pallas kernels for 31%

profile of v1, /device:TPU:39, one launch (start us, length us, event | category | flops | bytes accessed | tf_op | source)
XLA Modules:
  0.0 96.0 jit_solution(12986467563747071074)
XLA Ops:
  0.0 0.9 pad_maximum_fusion.2
  0.9 2.4 %all_gather.3.refs_3_ = bf16[640,256]{1,0:T(8,128)(2,1)S(1)} all-gather(bf16[320,256]{1,0:T(8,128)(2,1)S(1)} %pad_maximum_fusion.2), channel_id=1, replica_groups={{0,32},{64,96},{128,160},{192,224},{256,288},{320,352},{384,416},{448,4..., dimensions={0}, use_global_device_ids=true | all-gather | bytes 491520 | tf_op jit(solution)/shard_map/all_gather | solution.py:232
  3.3 10.6 %collective-permute-start = (bf16[640,256]{1,0:T(8,128)(2,1)S(1)}, bf16[640,256]{1,0:T(8,128)(2,1)S(1)}, u32[]{:S(2)}, u32[]{:S(2)}) collective-permute-start(bf16[640,256]{1,0:T(8,128)(2,1)S(1)} %all_gather.3.refs_3_), channel_id=1, source_target_pairs={{0,128},{32,416},{64,192},{96,480},{128,256},{160,32},{192,320},{2... | collective-permute-start | bytes 983048 | tf_op jit(solution)/shard_map/ppermute | solution.py:244
  14.0 2.2 %collective-permute-start.1 = (bf16[640,256]{1,0:T(8,128)(2,1)S(1)}, bf16[640,256]{1,0:T(8,128)(2,1)S(1)}, u32[]{:S(2)}, u32[]{:S(2)}) collective-permute-start(bf16[640,256]{1,0:T(8,128)(2,1)S(1)} %all_gather.3.refs_3_), channel_id=1, source_target_pairs={{0,64},{32,480},{64,128},{96,32},{128,192},{160,96},{192,256},{224... | collective-permute-start | bytes 983048 | tf_op jit(solution)/shard_map/ppermute | solution.py:244
  16.1 0.0 copy-start
  16.2 1.1 %copy-done = bf16[320,1024]{1,0:T(8,128)(2,1)S(1)} copy-done((bf16[320,1024]{1,0:T(8,128)(2,1)S(1)}, bf16[320,1024]{1,0:T(8,128)(2,1)}, u32[]{:S(2)}) %copy-start) | copy-done | bytes 655384
  17.2 0.0 copy-start.1
  17.2 0.7 copy-done.1
  17.9 18.5 %shard_map.46 = (bf16[2560,128]{1,0:T(8,128)(2,1)S(1)}, f32[16,1280]{1,0:T(8,128)S(1)}, f32[1,2560]{1,0:T(1,128)S(1)}, f32[144,2560]{1,0:T(8,128)S(1)}) custom-call(s32[1]{0:T(128)} %bitcast.refs_0_, s32[32]{0:T(128)S(1)} %copy-done.1, bf16[320,1024]{1,0:T(8,128)(2,1)S(1)} %copy-done, bf16[640,256]{1,0:T(8,128)(2,1)S(1)} %all_gather.3.refs_3_), custom_call_target="tpu_custom_call" | custom-call | flops 1 | bytes 1 | tf_op jit(solution)/shard_map/pallas_call | solution.py:216
  36.4 0.0 collective-permute-done.refs_4_
  36.5 1.9 %shard_map.47 = (f32[1,2560]{1,0:T(1,128)S(1)}, f32[144,2560]{1,0:T(8,128)S(1)}) custom-call(bf16[2560,128]{1,0:T(8,128)(2,1)S(1)} %get-tuple-element.25.refs_0_, f32[16,1280]{1,0:T(8,128)S(1)} %get-tuple-element.26.refs_1_, f32[1,2560]{1,0:T(1,128)S(1)} %get-tuple-element.27.refs_2_, f32[144,2560]{1,0:T(8,128)S(1)} %get-tuple-element.28.refs_3_, ...), custom_call_target="tpu_custom_call" | custom-call | flops 1 | bytes 1 | tf_op jit(solution)/shard_map/pallas_call | solution.py:216
  38.3 0.0 collective-permute-done.1.refs_4_
  38.4 1.9 %collective-permute-start.2 = (bf16[1280,256]{1,0:T(8,128)(2,1)S(1)}, bf16[1280,256]{1,0:T(8,128)(2,1)S(1)}, u32[]{:S(2)}, u32[]{:S(2)}) collective-permute-start(bf16[1280,256]{1,0:T(8,128)(2,1)S(1)} %pad_maximum_fusion), channel_id=1, source_target_pairs={{0,32},{32,0},{64,96},{96,64},{128,160},{160,128},{192,224},{224,1... | collective-permute-start | bytes 1966088 | tf_op jit(solution)/shard_map/ppermute | solution.py:236
  40.3 2.2 %collective-permute-start.3 = (bf16[640,256]{1,0:T(8,128)(2,1)S(1)}, bf16[640,256]{1,0:T(8,128)(2,1)S(1)}, u32[]{:S(2)}, u32[]{:S(2)}) collective-permute-start(bf16[640,256]{1,0:T(8,128)(2,1)S(1)} %collective-permute-done.refs_4_), channel_id=1, source_target_pairs={{0,64},{32,480},{64,128},{96,32},{128,192},{160,96},{192,256},{224... | collective-permute-start | bytes 983048 | tf_op jit(solution)/shard_map/ppermute | solution.py:244
  42.5 1.8 %shard_map.48 = (f32[1,2560]{1,0:T(1,128)S(1)}, f32[144,2560]{1,0:T(8,128)S(1)}) custom-call(bf16[2560,128]{1,0:T(8,128)(2,1)S(1)} %get-tuple-element.25.refs_0_, f32[16,1280]{1,0:T(8,128)S(1)} %get-tuple-element.26.refs_1_, f32[1,2560]{1,0:T(1,128)S(1)} %get-tuple-element.30.refs_2_, f32[144,2560]{1,0:T(8,128)S(1)} %get-tuple-element.31.refs_3_, ...), custom_call_target="tpu_custom_call" | custom-call | flops 1 | bytes 1 | tf_op jit(solution)/shard_map/pallas_call | solution.py:216
  44.3 0.0 collective-permute-done.2.refs_4_
  44.4 3.1 %shard_map.49 = (f32[1,2560]{1,0:T(1,128)S(1)}, f32[144,2560]{1,0:T(8,128)S(1)}) custom-call(bf16[2560,128]{1,0:T(8,128)(2,1)S(1)} %get-tuple-element.25.refs_0_, f32[16,1280]{1,0:T(8,128)S(1)} %get-tuple-element.26.refs_1_, f32[1,2560]{1,0:T(1,128)S(1)} %get-tuple-element.33.refs_2_, f32[144,2560]{1,0:T(8,128)S(1)} %get-tuple-element.34.refs_3_, ...), custom_call_target="tpu_custom_call" | custom-call | flops 1 | bytes 1 | tf_op jit(solution)/shard_map/pallas_call | solution.py:216
  47.5 1.0 collective-permute-done.3.refs_4_
  48.4 4.5 %collective-permute-start.4 = (bf16[640,256]{1,0:T(8,128)(2,1)S(1)}, bf16[640,256]{1,0:T(8,128)(2,1)S(1)}, u32[]{:S(2)}, u32[]{:S(2)}) collective-permute-start(bf16[640,256]{1,0:T(8,128)(2,1)S(1)} %collective-permute-done.3.refs_4_), channel_id=1, source_target_pairs={{0,32},{32,0},{64,96},{96,64},{128,160},{160,128},{192,224},{224,1... | collective-permute-start | bytes 983048 | tf_op jit(solution)/shard_map/ppermute | solution.py:236
  52.9 1.9 %collective-permute-start.5 = (bf16[320,256]{1,0:T(8,128)(2,1)S(1)}, bf16[320,256]{1,0:T(8,128)(2,1)S(1)}, u32[]{:S(2)}, u32[]{:S(2)}) collective-permute-start(bf16[320,256]{1,0:T(8,128)(2,1)S(1)} %constant_dynamic-slice_fusion), channel_id=1, source_target_pairs={{0,128},{32,416},{64,192},{96,480},{128,256},{160,32},{192,320},{2... | collective-permute-start | bytes 491528 | tf_op jit(solution)/shard_map/ppermute | solution.py:244
  54.9 2.0 %shard_map.50 = (f32[1,2560]{1,0:T(1,128)S(1)}, f32[144,2560]{1,0:T(8,128)S(1)}) custom-call(bf16[2560,128]{1,0:T(8,128)(2,1)S(1)} %get-tuple-element.25.refs_0_, f32[16,1280]{1,0:T(8,128)S(1)} %get-tuple-element.26.refs_1_, f32[1,2560]{1,0:T(1,128)S(1)} %get-tuple-element.36.refs_2_, f32[144,2560]{1,0:T(8,128)S(1)} %get-tuple-element.37.refs_3_, ...), custom_call_target="tpu_custom_call" | custom-call | flops 1 | bytes 1 | tf_op jit(solution)/shard_map/pallas_call | solution.py:216
  56.9 31.9 %collective-permute-done.5 = bf16[320,256]{1,0:T(8,128)(2,1)S(1)} collective-permute-done((bf16[320,256]{1,0:T(8,128)(2,1)S(1)}, bf16[320,256]{1,0:T(8,128)(2,1)S(1)}, u32[]{:S(2)}, u32[]{:S(2)}) %collective-permute-start.5) | collective-permute-done | bytes 163872 | tf_op jit(solution)/shard_map/ppermute | solution.py:244
  88.8 2.3 %collective-permute-start.6 = (bf16[320,256]{1,0:T(8,128)(2,1)S(1)}, bf16[320,256]{1,0:T(8,128)(2,1)S(1)}, u32[]{:S(2)}, u32[]{:S(2)}) collective-permute-start(bf16[320,256]{1,0:T(8,128)(2,1)S(1)} %collective-permute-done.5), channel_id=1, source_target_pairs={{0,32},{32,0},{64,96},{96,64},{128,160},{160,128},{192,224},{224,1... | collective-permute-start | bytes 491528 | tf_op jit(solution)/shard_map/ppermute | solution.py:236
  91.1 0.0 collective-permute-done.4
  91.1 2.6 %shard_map.51 = (f32[1,2560]{1,0:T(1,128)S(1)}, f32[144,2560]{1,0:T(8,128)S(1)}) custom-call(bf16[2560,128]{1,0:T(8,128)(2,1)S(1)} %get-tuple-element.25.refs_0_, f32[16,1280]{1,0:T(8,128)S(1)} %get-tuple-element.26.refs_1_, f32[1,2560]{1,0:T(1,128)S(1)} %get-tuple-element.39.refs_2_, f32[144,2560]{1,0:T(8,128)S(1)} %get-tuple-element.40.refs_3_, ...), custom_call_target="tpu_custom_call" | custom-call | flops 1 | bytes 1 | tf_op jit(solution)/shard_map/pallas_call | solution.py:216
  93.7 0.0 collective-permute-done.6.refs_4_
  93.7 2.3 %shard_map.52 = bf16[320,1024]{1,0:T(8,128)(2,1)} custom-call(bf16[2560,128]{1,0:T(8,128)(2,1)S(1)} %get-tuple-element.25.refs_0_, f32[16,1280]{1,0:T(8,128)S(1)} %get-tuple-element.26.refs_1_, f32[1,2560]{1,0:T(1,128)S(1)} %get-tuple-element.43.refs_2_, f32[144,2560]{1,0:T(8,128)S(1)} %get-tuple-element.44.refs_3_, ...), custom_call_target="tpu_custom_call" | custom-call | flops 1 | bytes 1 | tf_op jit(solution)/shard_map/pallas_call | solution.py:216
  (3 shorter events, 0.1 us)
Async XLA Ops:
  3.3 33.1 %collective-permute-start = (bf16[640,256]{1,0:T(8,128)(2,1)S(1)}, bf16[640,256]{1,0:T(8,128)(2,1)S(1)}, u32[]{:S(2)}, u32[]{:S(2)}) collective-permute-start(bf16[640,256]{1,0:T(8,128)(2,1)S(1)} %all_gather.3.refs_3_), channel_id=1, source_target_pairs={{0,128},{32,416},{64,192},{96,480},{128,256},{160,32},{192,320},{2... | collective-permute-start | bytes 983048 | tf_op jit(solution)/shard_map/ppermute | solution.py:244
  14.0 24.4 %collective-permute-start.1 = (bf16[640,256]{1,0:T(8,128)(2,1)S(1)}, bf16[640,256]{1,0:T(8,128)(2,1)S(1)}, u32[]{:S(2)}, u32[]{:S(2)}) collective-permute-start(bf16[640,256]{1,0:T(8,128)(2,1)S(1)} %all_gather.3.refs_3_), channel_id=1, source_target_pairs={{0,64},{32,480},{64,128},{96,32},{128,192},{160,96},{192,256},{224... | collective-permute-start | bytes 983048 | tf_op jit(solution)/shard_map/ppermute | solution.py:244
  16.1 1.1 %copy-start = (bf16[320,1024]{1,0:T(8,128)(2,1)S(1)}, bf16[320,1024]{1,0:T(8,128)(2,1)}, u32[]{:S(2)}) copy-start(bf16[320,1024]{1,0:T(8,128)(2,1)} %refs_2_.1) | copy-start | bytes 1966084
  17.2 0.7 copy-start.1
  38.4 6.0 %collective-permute-start.2 = (bf16[1280,256]{1,0:T(8,128)(2,1)S(1)}, bf16[1280,256]{1,0:T(8,128)(2,1)S(1)}, u32[]{:S(2)}, u32[]{:S(2)}) collective-permute-start(bf16[1280,256]{1,0:T(8,128)(2,1)S(1)} %pad_maximum_fusion), channel_id=1, source_target_pairs={{0,32},{32,0},{64,96},{96,64},{128,160},{160,128},{192,224},{224,1... | collective-permute-start | bytes 1966088 | tf_op jit(solution)/shard_map/ppermute | solution.py:236
  40.3 8.1 %collective-permute-start.3 = (bf16[640,256]{1,0:T(8,128)(2,1)S(1)}, bf16[640,256]{1,0:T(8,128)(2,1)S(1)}, u32[]{:S(2)}, u32[]{:S(2)}) collective-permute-start(bf16[640,256]{1,0:T(8,128)(2,1)S(1)} %collective-permute-done.refs_4_), channel_id=1, source_target_pairs={{0,64},{32,480},{64,128},{96,32},{128,192},{160,96},{192,256},{224... | collective-permute-start | bytes 983048 | tf_op jit(solution)/shard_map/ppermute | solution.py:244
  48.4 42.7 %collective-permute-start.4 = (bf16[640,256]{1,0:T(8,128)(2,1)S(1)}, bf16[640,256]{1,0:T(8,128)(2,1)S(1)}, u32[]{:S(2)}, u32[]{:S(2)}) collective-permute-start(bf16[640,256]{1,0:T(8,128)(2,1)S(1)} %collective-permute-done.3.refs_4_), channel_id=1, source_target_pairs={{0,32},{32,0},{64,96},{96,64},{128,160},{160,128},{192,224},{224,1... | collective-permute-start | bytes 983048 | tf_op jit(solution)/shard_map/ppermute | solution.py:236
  52.9 35.8 %collective-permute-start.5 = (bf16[320,256]{1,0:T(8,128)(2,1)S(1)}, bf16[320,256]{1,0:T(8,128)(2,1)S(1)}, u32[]{:S(2)}, u32[]{:S(2)}) collective-permute-start(bf16[320,256]{1,0:T(8,128)(2,1)S(1)} %constant_dynamic-slice_fusion), channel_id=1, source_target_pairs={{0,128},{32,416},{64,192},{96,480},{128,256},{160,32},{192,320},{2... | collective-permute-start | bytes 491528 | tf_op jit(solution)/shard_map/ppermute | solution.py:244
  88.8 5.0 %collective-permute-start.6 = (bf16[320,256]{1,0:T(8,128)(2,1)S(1)}, bf16[320,256]{1,0:T(8,128)(2,1)S(1)}, u32[]{:S(2)}, u32[]{:S(2)}) collective-permute-start(bf16[320,256]{1,0:T(8,128)(2,1)S(1)} %collective-permute-done.5), channel_id=1, source_target_pairs={{0,32},{32,0},{64,96},{96,64},{128,160},{160,128},{192,224},{224,1... | collective-permute-start | bytes 491528 | tf_op jit(solution)/shard_map/ppermute | solution.py:236
